TPU v7x, 32 devices: a whole 2x2x4 slice. The times are simulated.
32 devices in a mesh: grp: 2 (over x), ch: 16 (over z, y, core).
Axes of the slice: x: 2, y: 2, z: 4, core: 2. Of those that a mesh axis runs over, the one named last changes fastest.
Arguments:
- features: bfloat16 [2048, 2048], P('ch', 'grp'), parts along dimension 1, may hold values from -50 to 50
- dw_weight: float32 [2048, 49], P('ch'), may hold values from -0.875 to 0.875
- norm_gain: float32 [2048], replicated, may hold values from 0.25 to 1.75
- layer_scale: float32 [2048], replicated, may hold values from 0.2 to 1
- w_in: bfloat16 [8192, 2048], P('ch'), may hold values from -0.125 to 0.125
- w_out: bfloat16 [8192, 2048], P('ch'), may hold values from -0.0625 to 0.0625
- w_head: bfloat16 [2048, 150], replicated, may hold values from -3 to 3
- labels: int32 [2048], P('grp'), parts along dimension 0, may hold values from 0 to 149
Outputs:
- d_features: float32 [2048, 2048], P('ch', 'grp'), parts along dimension 1
- d_dw: float32 [2048, 98], P('ch', 'grp'), parts along dimension 1
- d_scale: float32 [4096], P(('grp', 'ch')), parts along dimension 0
- d_w_in: float32 [16384, 2048], P(('grp', 'ch')), parts along dimension 0
- d_w_out: float32 [16384, 2048], P(('grp', 'ch')), parts along dimension 0
- d_head: float32 [2048, 300], P('ch', 'grp'), parts along dimension 1
- mean_loss: float32 [2], P('grp'), parts along dimension 0
There are 2 independent parts, one for each index of `grp`. A program takes and returns all parts, laid end to end along the dimension named above; an argument that names none is the same for every part. Nothing has to cross between parts.
All inputs are finite; a program needn't handle non-finite values.
Results may differ from a plain program's by a relative error of at most 0.012.
Values may be sent and summed in bfloat16 or wider, within the bound.
A program may use at most 128 MiB of HBM per device.

v0:
```python
import jax
import jax.numpy as jnp
from jax import lax
from jax.sharding import PartitionSpec as P

KS = 7
WIN_H = 32
WIN_W = 32
norm_eps = 1e-06


def conv_apply(in_grid, kernel):
    half = KS // 2
    padded = jnp.pad(in_grid, ((0, 0), (half, half), (half, half)))
    running = jnp.zeros(in_grid.shape, in_grid.dtype)
    for row_shift in range(KS):
        for col_shift in range(KS):
            tap = kernel[:, row_shift * KS + col_shift]
            running = (
                running
                + tap[:, None, None]
                * padded[:, row_shift : row_shift + WIN_H, col_shift : col_shift + WIN_W]
            )
    return running


def gelu_parts(values):
    cum_prob = 0.5 * (1.0 + lax.erf(values * 0.7071067811865476))
    density = jnp.exp(-0.5 * values * values) * 0.3989422804014327
    return (values * cum_prob, cum_prob + values * density)


def per_device(features, dw_weight, norm_gain, layer_scale, w_in, w_out, w_head, labels):
    highest = lax.Precision.HIGHEST
    my_rows = features.shape[0]
    tok_count = features.shape[1]
    class_count = w_head.shape[1]
    row_offset = lax.axis_index("ch") * my_rows
    inputs_wide = features.astype(jnp.float32)
    in_grid = inputs_wide.reshape(my_rows, WIN_H, WIN_W)
    conv_out = conv_apply(in_grid, dw_weight).reshape(my_rows, tok_count).astype(jnp.bfloat16)
    conv_all = lax.all_gather(conv_out, "ch", axis=0, tiled=True)
    conv_wide = conv_all.astype(jnp.float32)
    tok_mean = jnp.mean(conv_wide, axis=0)
    centered = conv_wide - tok_mean[None, :]
    tok_var = jnp.mean(centered * centered, axis=0)
    inv_std = 1.0 / jnp.sqrt(tok_var + norm_eps)
    normed = centered * inv_std[None, :]
    norm_out = (norm_gain[:, None] * normed).astype(jnp.bfloat16)
    pre_act = jnp.dot(w_in, norm_out, preferred_element_type=jnp.float32)
    gelu_out, gelu_slope = gelu_parts(pre_act)
    hidden = gelu_out.astype(jnp.bfloat16)
    my_scale = lax.dynamic_slice_in_dim(layer_scale, row_offset, my_rows, 0)
    head_wide = w_head.astype(jnp.float32)
    my_head = lax.dynamic_slice_in_dim(head_wide, row_offset, my_rows, 0)
    w_cols = w_out
    branch_sum = lax.psum_scatter(
        lax.dot_general(
            w_cols, hidden, (((0,), (0,)), ((), ())), preferred_element_type=jnp.float32
        ),
        "ch",
        scatter_dimension=0,
        tiled=True,
    )
    block_out = inputs_wide + my_scale[:, None] * branch_sum
    part_logits = lax.dot_general(block_out, my_head, (((0,), (0,)), ((), ())), precision=highest)
    logits = lax.psum(part_logits, "ch")
    row_max = jnp.max(logits, axis=1, keepdims=True)
    exp_terms = jnp.exp(logits - row_max)
    exp_total = jnp.sum(exp_terms, axis=1, keepdims=True)
    log_total = jnp.log(exp_total) + row_max
    onehot = (labels[:, None] == jnp.arange(class_count, dtype=jnp.int32)[None, :]).astype(
        jnp.float32
    )
    picked = jnp.sum(logits * onehot, axis=1)
    mean_loss = jnp.mean(log_total[:, 0] - picked).reshape(1)
    logit_grad = exp_terms / exp_total - onehot
    out_grad = lax.dot_general(my_head, logit_grad, (((1,), (1,)), ((), ())), precision=highest)
    d_head = jnp.dot(block_out, logit_grad, precision=highest)
    d_scale = jnp.sum(out_grad * branch_sum, axis=1)
    branch_grad = (my_scale[:, None] * out_grad).astype(jnp.bfloat16)
    incoming = lax.all_gather(branch_grad, "ch", axis=0, tiled=True)
    w_cols = w_out
    hidden_acc = jnp.dot(w_cols, incoming, preferred_element_type=jnp.float32)
    tile_grad = lax.dot_general(
        hidden, incoming, (((1,), (1,)), ((), ())), preferred_element_type=jnp.float32
    )
    pre_grad = (hidden_acc * gelu_slope).astype(jnp.bfloat16)
    d_w_in = lax.dot_general(
        pre_grad, norm_out, (((1,), (1,)), ((), ())), preferred_element_type=jnp.float32
    )
    norm_grad = lax.dot_general(
        w_in, pre_grad, (((0,), (0,)), ((), ())), preferred_element_type=jnp.float32
    )
    gained = norm_gain[:, None] * norm_grad
    conv_term = (
        gained
        - jnp.mean(gained, axis=0)[None, :]
        - normed * jnp.mean(gained * normed, axis=0)[None, :]
    ) * inv_std[None, :]
    conv_grad = lax.psum_scatter(conv_term, "ch", scatter_dimension=0, tiled=True)
    unused, pullback = jax.vjp(conv_apply, in_grid, dw_weight)
    grid_grad, d_dw = pullback(conv_grad.reshape(my_rows, WIN_H, WIN_W))
    d_features = out_grad + grid_grad.reshape(my_rows, tok_count)
    return (d_features, d_dw, d_scale, d_w_in, tile_grad, d_head, mean_loss)


def solution(mesh):
    placed = (P("ch", "grp"), P("ch", None), P(), P(), P("ch", None), P("ch", None), P(), P("grp"))
    return jax.shard_map(
        per_device,
        mesh=mesh,
        in_specs=placed,
        out_specs=(
            P("ch", "grp"),
            P("ch", "grp"),
            P(("grp", "ch")),
            P(("grp", "ch"), None),
            P(("grp", "ch"), None),
            P("ch", "grp"),
            P("grp"),
        ),
        check_vma=False,
    )
```

profile of v0, /device:TPU:0, one launch (start us, length us, event | category | flops | bytes accessed | tf_op | source)
XLA Modules:
  0.0 497.7 jit_solution(14007070145774544614)
XLA Ops:
  7.2 0.0 copy-start
  7.2 0.0 all-gather.3.cloned.1.call-start
  7.2 1.0 slice_bitcast_fusion.46
  8.2 1.0 slice_bitcast_fusion.48
  9.2 0.0 copy-start.28
  9.2 0.0 copy-start.29
  9.2 0.0 copy-start.30
  9.3 1.0 slice_bitcast_fusion.47
  10.4 1.1 copy.19
  11.5 0.1 bitcast_convert_fusion
  11.6 4.8 add_convert_fusion
  16.4 0.0 all-gather.3.cloned.1.call-update
  16.4 0.0 copy-start.13
  16.4 0.0 reduce-scatter.3.cloned.1.call-start
  16.5 56.0 %all-gather.3.cloned.1.call-done = bf16[2048,1024]{0,1:T(8,128)(2,1)} async-done(((bf16[128,1024]{0,1:T(8,128)(2,1)}), bf16[2048,1024]{0,1:T(8,128)(2,1)}) %all-gather.3.cloned.1.call-update) | async-done | bytes 4194320 | tf_op jit(solution)/shard_map/all_gather | solution.py:42
  72.5 3.0 convert_reduce_fusion
  75.5 0.5 copy-done.2
  75.9 1.2 fusion.9
  77.3 1.6 fusion.5
  79.0 0.0 copy-start.4
  79.0 0.0 copy-start.45
  79.0 2.4 fusion.31
  81.4 1.3 copy-done.7
  82.7 5.6 %convolution_bitcast_fusion = f32[2048,1024]{0,1:T(8,128)} fusion(bf16[512,2048]{1,0:T(8,128)(2,1)S(1)} %copy-done.45, f32[1024,512]{1,0:T(8,128)S(1)} %fusion.31), kind=kOutput, calls=%fused_computation.62 | convolution fusion | flops 2150105088 | bytes 12582912 | tf_op jit(solution)/shard_map/dot_general | solution.py:58
  88.3 0.0 reduce-scatter.3.cloned.1.call-update
  88.4 0.0 all-reduce.101.cloned.1.call-start
  88.4 0.8 dynamic_slice.7
  89.2 102.4 %reduce-scatter.3.cloned.1.call-done = f32[128,1024]{0,1:T(8,128)} async-done(((f32[2048,1024]{0,1:T(8,128)}), f32[128,1024]{0,1:T(8,128)}) %reduce-scatter.3.cloned.1.call-update) | async-done | bytes 524304 | tf_op jit(solution)/shard_map/reduce_scatter | solution.py:57
  191.5 2.6 fusion.22
  194.1 0.0 all-reduce.101.cloned.1.call-update
  194.1 0.0 all-gather.5.cloned.1.call-start
  194.2 91.7 %all-reduce.101.cloned.1.call-done = f32[1024,150]{0,1:T(8,128)} async-done(((f32[1024,150]{0,1:T(8,128)}), f32[1024,150]{0,1:T(8,128)}) %all-reduce.101.cloned.1.call-update) | async-done | bytes 614416 | tf_op jit(solution)/shard_map/psum | solution.py:67
  285.9 1.1 reduce_max.9
  287.0 1.2 select_reduce_fusion
  288.2 1.7 fusion.23
  289.9 0.0 copy-start.11
  289.9 1.0 copy.20
  290.9 2.5 multiply_reduce_fusion.1
  293.4 0.0 all-gather.5.cloned.1.call-update
  293.4 0.2 reduce-scatter.5.cloned.1.call-start
  293.7 53.5 %all-gather.5.cloned.1.call-done = bf16[2048,1024]{0,1:T(8,128)(2,1)} async-done(((bf16[128,1024]{0,1:T(8,128)(2,1)}), bf16[2048,1024]{0,1:T(8,128)(2,1)}) %all-gather.5.cloned.1.call-update) | async-done | bytes 4194320 | tf_op jit(solution)/shard_map/all_gather | solution.py:82
  347.2 6.5 %fusion.15 = bf16[512,1024]{0,1:T(8,128)(2,1)S(1)} fusion(f32[1024,512]{1,0:T(8,128)} %copy-done.7, bf16[2048,1024]{0,1:T(8,128)(2,1)} %all-gather.5.cloned.1.call-done, bf16[512,2048]{1,0:T(8,128)(2,1)} %param.13), kind=kOutput, calls=%fused_computation.69 | convolution fusion | flops 2152726528 | bytes 9437184 | tf_op jit(solution)/shard_map/dot_general | solution.py:84
  353.7 3.0 fusion.6
  356.7 0.6 multiply_reduce_fusion
  357.3 5.4 %fusion.8 = f32[2048,1024]{0,1:T(8,128)} fusion(bf16[2048,1024]{0,1:T(8,128)(2,1)S(1)} %copy-done.3, f32[1024,2048]{1,0:T(8,128)S(1)} %get-tuple-element.158, f32[1024]{0:T(1024)S(1)} %get-tuple-element.159, f32[1024]{0:T(1024)S(1)} %get-tuple-element.160, f32[2048]{0:T(1024)S(1)} %copy-done.13, f32[1024]{0:T(1024)S(1)} %add_rsqrt_fusion, ...), kind=kLoop, calls=%fused_computation.10 | loop fusion | flops 16777216 | bytes 20996096 | tf_op jit(solution)/shard_map/mul | solution.py:96
  362.8 0.0 reduce-scatter.5.cloned.1.call-update
  362.8 0.6 subtract_reduce_fusion
  364.1 1.5 fusion.21
  365.6 7.4 %fusion.32 = f32[512,2048]{1,0:T(8,128)} fusion(bf16[512,1024]{0,1:T(8,128)(2,1)} %copy-done.10, bf16[2048,1024]{0,1:T(8,128)(2,1)} %copy-done.4), kind=kOutput, calls=%fused_computation.255 | convolution fusion | flops 2147483648 | bytes 9437184 | tf_op jit(solution)/shard_map/dot_general | solution.py:89
  372.9 4.5 fusion.28
  377.5 88.5 %reduce-scatter.5.cloned.1.call-done = f32[128,1024]{0,1:T(8,128)} async-done(((f32[2048,1024]{0,1:T(8,128)}), f32[128,1024]{0,1:T(8,128)}) %reduce-scatter.5.cloned.1.call-update) | async-done | bytes 524304 | tf_op jit(solution)/shard_map/reduce_scatter | solution.py:101
  465.9 2.9 broadcast_multiply_fusion.2
  468.9 1.1 broadcast_multiply_fusion.1
  470.0 2.4 broadcast_multiply_fusion
  472.4 6.0 %pad_add_fusion = f32[128,38,38]{0,2,1:T(8,128)S(1)} fusion(f32[128,32,32]{0,2,1:T(8,128)S(1)} %get-tuple-element.66, f32[128,32,32]{0,2,1:T(8,128)S(1)} %get-tuple-element.67, f32[128,32,32]{0,2,1:T(8,128)S(1)} %get-tuple-element.68, f32[128,32,32]{0,2,1:T(8,128)S(1)} %get-tuple-element.69, f32[128,32,32]{0,2,1:T(8,128)S(1)} %get-tuple-element.70, ...), kind=kLoop, calls=%fused_computation.76 | loop fusion | flops 7762944 | bytes 23283712 | tf_op jit(solution)/shard_map/transpose(jvp())/add_any | solution.py:22
  478.4 0.0 copy-start.1
  478.4 3.1 pad_add_fusion.1
  481.5 2.1 copy.21
  483.5 2.1 add.438
  485.6 0.2 multiply_reduce_fusion.26
  485.8 0.6 multiply_reduce_fusion.48
  486.4 1.4 multiply_reduce_fusion.49
  487.8 1.4 multiply_reduce_fusion.50
  489.2 0.8 pad_add_fusion.7
  (84 shorter events, 0.2 us)
Async XLA Ops:
  7.2 71.8 %copy-start = (bf16[512,2048]{1,0:T(8,128)(2,1)S(1)}, bf16[512,2048]{1,0:T(8,128)(2,1)}, u32[]{:S(2)}) copy-start(bf16[512,2048]{1,0:T(8,128)(2,1)} %param.12) | copy-start | bytes 6291460
  7.2 65.3 %all-gather.3.cloned.1.call-start = ((), (), s32[]{:S(2)}) async-start(), calls=%async_computation.2 | async-start | bytes 4456448 | tf_op jit(solution)/shard_map/all_gather | solution.py:42
  9.2 7.3 %copy-start.28 = (f32[128]{0:T(128)}, f32[128]{0:T(128)S(1)}, u32[]{:S(2)}) copy-start(f32[128]{0:T(128)S(1)} %get-tuple-element.109) | copy-start | bytes 1540
  9.2 67.9 %copy-start.29 = (f32[128]{0:T(128)}, f32[128]{0:T(128)S(1)}, u32[]{:S(2)}) copy-start(f32[128]{0:T(128)S(1)} %get-tuple-element.110) | copy-start | bytes 1540
  9.2 67.9 %copy-start.30 = (f32[128]{0:T(128)}, f32[128]{0:T(128)S(1)}, u32[]{:S(2)}) copy-start(f32[128]{0:T(128)S(1)} %get-tuple-element.111) | copy-start | bytes 1540
  9.2 67.9 %copy-start.31 = (f32[128]{0:T(128)}, f32[128]{0:T(128)S(1)}, u32[]{:S(2)}) copy-start(f32[128]{0:T(128)S(1)} %get-tuple-element.112) | copy-start | bytes 1540
  9.2 67.9 %copy-start.32 = (f32[128]{0:T(128)}, f32[128]{0:T(128)S(1)}, u32[]{:S(2)}) copy-start(f32[128]{0:T(128)S(1)} %get-tuple-element.113) | copy-start | bytes 1540
  9.3 67.9 %copy-start.33 = (f32[128]{0:T(128)}, f32[128]{0:T(128)S(1)}, u32[]{:S(2)}) copy-start(f32[128]{0:T(128)S(1)} %get-tuple-element.114) | copy-start | bytes 1540
  9.3 67.9 %copy-start.34 = (f32[128]{0:T(128)}, f32[128]{0:T(128)S(1)}, u32[]{:S(2)}) copy-start(f32[128]{0:T(128)S(1)} %get-tuple-element.115) | copy-start | bytes 1540
  9.3 67.9 %copy-start.35 = (f32[128]{0:T(128)}, f32[128]{0:T(128)S(1)}, u32[]{:S(2)}) copy-start(f32[128]{0:T(128)S(1)} %get-tuple-element.116) | copy-start | bytes 1540
  9.3 67.9 %copy-start.36 = (f32[128]{0:T(128)}, f32[128]{0:T(128)S(1)}, u32[]{:S(2)}) copy-start(f32[128]{0:T(128)S(1)} %get-tuple-element.117) | copy-start | bytes 1540
  9.3 67.9 %copy-start.37 = (f32[128]{0:T(128)}, f32[128]{0:T(128)S(1)}, u32[]{:S(2)}) copy-start(f32[128]{0:T(128)S(1)} %get-tuple-element.118) | copy-start | bytes 1540
  9.3 67.9 %copy-start.38 = (f32[128]{0:T(128)}, f32[128]{0:T(128)S(1)}, u32[]{:S(2)}) copy-start(f32[128]{0:T(128)S(1)} %get-tuple-element.119) | copy-start | bytes 1540
  9.3 67.9 %copy-start.39 = (f32[128]{0:T(128)}, f32[128]{0:T(128)S(1)}, u32[]{:S(2)}) copy-start(f32[128]{0:T(128)S(1)} %get-tuple-element.120) | copy-start | bytes 1540
  9.3 67.9 %copy-start.40 = (f32[128]{0:T(128)}, f32[128]{0:T(128)S(1)}, u32[]{:S(2)}) copy-start(f32[128]{0:T(128)S(1)} %get-tuple-element.121) | copy-start | bytes 1540
  10.3 6.0 %copy-start.14 = (f32[128]{0:T(128)}, f32[128]{0:T(128)S(1)}, u32[]{:S(2)}) copy-start(f32[128]{0:T(128)S(1)} %get-tuple-element.133) | copy-start | bytes 1540
  10.3 6.0 %copy-start.16 = (f32[128]{0:T(128)}, f32[128]{0:T(128)S(1)}, u32[]{:S(2)}) copy-start(f32[128]{0:T(128)S(1)} %get-tuple-element.134) | copy-start | bytes 1540
  10.4 62.1 %copy-start.18 = (f32[128]{0:T(128)}, f32[128]{0:T(128)S(1)}, u32[]{:S(2)}) copy-start(f32[128]{0:T(128)S(1)} %get-tuple-element.135) | copy-start | bytes 1540
  10.4 65.1 %copy-start.20 = (f32[128]{0:T(128)}, f32[128]{0:T(128)S(1)}, u32[]{:S(2)}) copy-start(f32[128]{0:T(128)S(1)} %get-tuple-element.136) | copy-start | bytes 1540
  10.4 65.1 %copy-start.22 = (f32[128]{0:T(128)}, f32[128]{0:T(128)S(1)}, u32[]{:S(2)}) copy-start(f32[128]{0:T(128)S(1)} %get-tuple-element.137) | copy-start | bytes 1540
  10.4 66.9 %copy-start.24 = (f32[128]{0:T(128)}, f32[128]{0:T(128)S(1)}, u32[]{:S(2)}) copy-start(f32[128]{0:T(128)S(1)} %get-tuple-element.138) | copy-start | bytes 1540
  10.4 66.9 %copy-start.26 = (f32[128]{0:T(128)}, f32[128]{0:T(128)S(1)}, u32[]{:S(2)}) copy-start(f32[128]{0:T(128)S(1)} %get-tuple-element.139) | copy-start | bytes 1540
  16.4 60.9 %copy-start.13 = (f32[2048]{0:T(1024)S(1)}, f32[2048]{0:T(1024)}, u32[]{:S(2)}) copy-start(f32[2048]{0:T(1024)} %param.10) | copy-start | bytes 24580
  16.4 175.1 %reduce-scatter.3.cloned.1.call-start = ((), (), s32[]{:S(2)}) async-start(), calls=%async_computation.3 | async-start | bytes 8912896 | tf_op jit(solution)/shard_map/reduce_scatter | solution.py:57
  72.5 3.4 copy-start.2
  79.0 2.4 copy-start.4
  79.0 3.8 copy-start.45
  81.4 1.4 copy-start.7
  88.3 198.7 %copy-start.41 = (s32[1024]{0:T(1024)S(1)}, s32[1024]{0:T(1024)}, u32[]{:S(2)}) copy-start(s32[1024]{0:T(1024)} %param.15) | copy-start | bytes 12292
  88.4 197.5 %all-reduce.101.cloned.1.call-start = ((), (), s32[]{:S(2)}) async-start(), calls=%async_computation.4 | async-start | bytes 1245184 | tf_op jit(solution)/shard_map/psum | solution.py:67
  89.2 105.0 %copy-start.43 = (f32[128]{0:T(128)}, f32[128]{0:T(128)S(1)}, u32[]{:S(2)}) copy-start(f32[128]{0:T(128)S(1)} %dynamic_slice.7) | copy-start | bytes 1540
  194.1 153.1 %all-gather.5.cloned.1.call-start = ((), (), s32[]{:S(2)}) async-start(), calls=%async_computation.5 | async-start | bytes 4456448 | tf_op jit(solution)/shard_map/all_gather | solution.py:82
  289.9 63.7 %copy-start.11 = (f32[128,1024]{1,0:T(8,128)}, f32[128,1024]{1,0:T(8,128)S(1)}, u32[]{:S(2)}) copy-start(f32[128,1024]{1,0:T(8,128)S(1)} %fusion.23) | copy-start | bytes 1572868
  293.4 172.5 %reduce-scatter.5.cloned.1.call-start = ((), (), s32[]{:S(2)}) async-start(), calls=%async_computation.6 | async-start | bytes 8912896 | tf_op jit(solution)/shard_map/reduce_scatter | solution.py:101
  347.2 6.5 %copy-start.3 = (bf16[2048,1024]{0,1:T(8,128)(2,1)S(1)}, bf16[2048,1024]{0,1:T(8,128)(2,1)}, u32[]{:S(2)}) copy-start(bf16[2048,1024]{0,1:T(8,128)(2,1)} %all-gather.3.cloned.1.call-done) | copy-start | bytes 12582916
  353.7 3.0 copy-start.10
  362.8 1.3 copy-start.9
  362.8 1.3 copy-start.12
  362.8 1.3 copy-start.42
  362.8 1.3 copy-start.44
  365.6 7.4 %copy-start.6 = (bf16[2048,1024]{0,1:T(8,128)(2,1)S(1)}, bf16[2048,1024]{0,1:T(8,128)(2,1)}, u32[]{:S(2)}) copy-start(bf16[2048,1024]{0,1:T(8,128)(2,1)} %all-gather.5.cloned.1.call-done) | copy-start | bytes 12582916
  365.6 7.4 %copy-start.8 = (f32[1024,512]{1,0:T(8,128)S(1)}, f32[1024,512]{1,0:T(8,128)}, u32[]{:S(2)}) copy-start(f32[1024,512]{1,0:T(8,128)} %copy-done.7) | copy-start | bytes 6291460
  377.4 91.4 %copy-start.15 = (f32[128]{0:T(128)S(1)}, f32[128]{0:T(128)}, u32[]{:S(2)}) copy-start(f32[128]{0:T(128)} %copy-done.14) | copy-start | bytes 1540
  377.4 91.4 %copy-start.17 = (f32[128]{0:T(128)S(1)}, f32[128]{0:T(128)}, u32[]{:S(2)}) copy-start(f32[128]{0:T(128)} %copy-done.16) | copy-start | bytes 1540
  377.4 91.4 %copy-start.19 = (f32[128]{0:T(128)S(1)}, f32[128]{0:T(128)}, u32[]{:S(2)}) copy-start(f32[128]{0:T(128)} %copy-done.18) | copy-start | bytes 1540
  377.5 91.4 %copy-start.21 = (f32[128]{0:T(128)S(1)}, f32[128]{0:T(128)}, u32[]{:S(2)}) copy-start(f32[128]{0:T(128)} %copy-done.20) | copy-start | bytes 1540
  377.5 91.4 %copy-start.23 = (f32[128]{0:T(128)S(1)}, f32[128]{0:T(128)}, u32[]{:S(2)}) copy-start(f32[128]{0:T(128)} %copy-done.22) | copy-start | bytes 1540
  377.5 91.4 %copy-start.25 = (f32[128]{0:T(128)S(1)}, f32[128]{0:T(128)}, u32[]{:S(2)}) copy-start(f32[128]{0:T(128)} %copy-done.24) | copy-start | bytes 1540
  377.5 91.4 %copy-start.27 = (f32[128]{0:T(128)S(1)}, f32[128]{0:T(128)}, u32[]{:S(2)}) copy-start(f32[128]{0:T(128)} %copy-done.26) | copy-start | bytes 1540
  465.9 3.0 copy-start.5
  478.4 11.6 %copy-start.1 = (bf16[512,2048]{1,0:T(8,128)(2,1)S(1)}, bf16[512,2048]{1,0:T(8,128)(2,1)}, u32[]{:S(2)}) copy-start(bf16[512,2048]{1,0:T(8,128)(2,1)} %param.12) | copy-start | bytes 6291460
Sparse Core Ops, SparseCore 0:
  16.5 55.9 all-gather.2
  88.5 103.0 reduce-scatter.2
  195.5 90.2 all-reduce.100
  293.5 53.5 all-gather.4
  362.9 102.9 reduce-scatter.4
where the time goes:
time: 498 us
  waiting for transfers between devices  392 us (79%)
  other arithmetic  44 us (9%)
  matrix products  35 us (7%)
  between operations  16.2 us (3%)
  local copies, waits for them, and re-layouts  9.9 us (2%)
    reduce_scatter x1, waiting for transfers between devices, per_device(): lax.psum_scatter(lax.dot_general(w_cols, hidden, (((0,), (0,)), ((), ()))...  102 us
    psum x1, waiting for transfers between devices, per_device(): logits = lax.psum(part_logits, 'ch')  91.7 us
    reduce_scatter x1, waiting for transfers between devices, per_device(): lax.psum_scatter(conv_term, 'ch', scatter_dimension=0, tiled=True)  88.5 us
    all_gather x1, waiting for transfers between devices, per_device(): conv_all = lax.all_gather(conv_out, 'ch', axis=0, tiled=True)  56 us
    all_gather x1, waiting for transfers between devices, per_device(): incoming = lax.all_gather(branch_grad, 'ch', axis=0, tiled=True)  53.5 us
  transfers between devices with their start and end apart: 5, of which 5 were waited for; matrix products, arithmetic and copies ran while one was open for 3% of the time, Pallas kernels for 0%

commit v1 on v0

--- a/solution.py
+++ b/solution.py
@@ -7,6 +7,13 @@
 WIN_H = 32
 WIN_W = 32
 norm_eps = 1e-06
+
+
+def _make_ticks(t0, pos_dim):
+    base_arr = list(t0.shape[1:])
+    base_arr[pos_dim] *= t0.shape[0]
+    z1 = jnp.moveaxis(t0, 0, pos_dim).reshape(base_arr)
+    return z1
 
 
 def conv_apply(in_grid, kernel):
@@ -39,7 +46,21 @@
     inputs_wide = features.astype(jnp.float32)
     in_grid = inputs_wide.reshape(my_rows, WIN_H, WIN_W)
     conv_out = conv_apply(in_grid, dw_weight).reshape(my_rows, tok_count).astype(jnp.bfloat16)
-    conv_all = lax.all_gather(conv_out, "ch", axis=0, tiled=True)
+    n_slots = lax.axis_size("ch")
+    nodes = [(i0, (i0 + 1) % n_slots) for i0 in range(n_slots)]
+    copies = [(num, pp) for pp, num in nodes]
+    step_out, frame_out = ([], [])
+    j = 0
+    while j < n_slots - 1:
+        if j % 2 == 0:
+            step_out.append(lax.ppermute(step_out[-1] if step_out else conv_out, "ch", nodes))
+        else:
+            frame_out.append(lax.ppermute(frame_out[-1] if frame_out else conv_out, "ch", copies))
+        j += 1
+    side_arr = jnp.stack([*step_out[::-1], conv_out, *frame_out], axis=0)
+    state_next = lax.axis_index("ch") - len(step_out)
+    side_arr = side_arr[(jnp.arange(n_slots) - state_next) % n_slots]
+    conv_all = _make_ticks(side_arr, 0)
     conv_wide = conv_all.astype(jnp.float32)
     tok_mean = jnp.mean(conv_wide, axis=0)
     centered = conv_wide - tok_mean[None, :]

time: 498 us -> 551 us (1.11)
  local copies, waits for them, and re-layouts: 9.9 us -> 45.5 us
  starting transfers between devices: 0.39 us -> 33.3 us
  waiting for transfers between devices: 392 us -> 371 us
    all_gather x1 -> x0, waiting for transfers between devices: 56 us -> none  [per_device(): conv_all = lax.all_gather(conv_out, 'ch', axis=0, tiled=True)]
    ppermute x0 -> x15, waiting for transfers between devices: none -> 35.2 us  [the longest x8 29.8 us: per_device(): lax.ppermute(step_out[-1] if step_out else conv_out, 'ch', nodes)]
    ppermute x0 -> x15, starting transfers between devices: none -> 33.2 us  [the longest x7 32.7 us: per_device(): lax.ppermute(frame_out[-1] if frame_out else conv_out, 'ch', copies)]
    unnamed x93 -> x166, local copies, waits for them, and re-layouts: 3.12 us -> 24.9 us
    convert_element_type x0 -> x3, local copies, waits for them, and re-layouts: none -> 8.15 us  [the longest x1 7.15 us: per_device(): conv_wide = conv_all.astype(jnp.float32)]
  transfers between devices with their start and end apart: 5 -> 19, of which waited for: 5 -> 18; matrix products, arithmetic and copies ran while one was open for 3% -> 6% of each run, Pallas kernels for 0% -> 0%
where the time goes in v1:
time: 551 us; the launch traced here: 550 us
  waiting for transfers between devices  371 us (67%)
  local copies, waits for them, and re-layouts  45.5 us (8%)
  other arithmetic  45.4 us (8%)
  matrix products  37.6 us (7%)
  starting transfers between devices  33.3 us (6%)
  between operations  16.5 us (3%)
    reduce_scatter x1, waiting for transfers between devices, per_device(): lax.psum_scatter(lax.dot_general(w_cols, hidden, (((0,), (0,)), ((), ()))...  102 us
    psum x1, waiting for transfers between devices, per_device(): logits = lax.psum(part_logits, 'ch')  91.6 us
    reduce_scatter x1, waiting for transfers between devices, per_device(): lax.psum_scatter(conv_term, 'ch', scatter_dimension=0, tiled=True)  88.7 us
    all_gather x1, waiting for transfers between devices, per_device(): incoming = lax.all_gather(branch_grad, 'ch', axis=0, tiled=True)  53.7 us
    ppermute x7, starting transfers between devices, per_device(): lax.ppermute(frame_out[-1] if frame_out else conv_out, 'ch', copies)  32.7 us
    ppermute x8, waiting for transfers between devices, per_device(): lax.ppermute(step_out[-1] if step_out else conv_out, 'ch', nodes)  29.8 us
    unnamed x166, local copies, waits for them, and re-layouts  24.9 us
  transfers between devices with their start and end apart: 19, of which 18 were waited for; matrix products, arithmetic and copies ran while one was open for 6% of the time, Pallas kernels for 0%

profile of v1, /device:TPU:0, one launch (start us, length us, event | category | flops | bytes accessed | tf_op | source)
XLA Modules:
  0.0 549.7 jit_solution(16679705044943498053)
XLA Ops:
  8.2 1.0 slice_bitcast_fusion.48
  9.3 1.0 slice_bitcast_fusion.47
  10.4 1.1 copy.26
  11.6 4.1 add_convert_fusion
  17.1 9.3 %collective-permute-done = bf16[128,1024]{1,0:T(8,128)(2,1)S(1)} collective-permute-done((bf16[128,1024]{1,0:T(8,128)(2,1)}, bf16[128,1024]{1,0:T(8,128)(2,1)S(1)}, u32[]{:S(2)}, u32[]{:S(2)}) %collective-permute-start) | collective-permute-done | bytes 262176 | tf_op jit(solution)/shard_map/ppermute | solution.py:56
  26.4 4.4 collective-permute-start.8
  30.8 4.1 collective-permute-done.1
  35.7 4.6 collective-permute-start.9
  40.4 3.1 collective-permute-done.2
  44.2 4.7 collective-permute-start.10
  49.0 3.1 collective-permute-done.3
  52.9 4.7 collective-permute-start.11
  57.6 3.1 collective-permute-done.4
  62.2 4.7 collective-permute-start.12
  66.9 2.4 collective-permute-done.5
  69.3 1.5 collective-permute-done.12
  70.8 4.8 collective-permute-start.13
  75.6 2.4 collective-permute-done.6
  78.2 1.6 collective-permute-done.13
  79.8 4.7 collective-permute-start.14
  84.5 2.3 collective-permute-done.7
  86.8 1.7 bitcast_dynamic-update-slice_fusion.14
  88.5 1.7 bitcast_dynamic-update-slice_fusion.13
  90.2 1.7 bitcast_dynamic-update-slice_fusion.12
  91.8 1.7 bitcast_dynamic-update-slice_fusion.11
  93.5 1.7 bitcast_dynamic-update-slice_fusion.10
  95.2 1.7 bitcast_dynamic-update-slice_fusion.9
  96.8 1.7 bitcast_dynamic-update-slice_fusion.8
  98.5 1.7 bitcast_dynamic-update-slice_fusion.7
  103.8 1.7 bitcast_dynamic-update-slice_fusion.2
  105.5 1.7 bitcast_dynamic-update-slice_fusion.1
  107.9 5.0 gather_fusion
  112.9 3.0 convert_reduce_fusion
  116.4 1.1 multiply_reduce_fusion
  117.5 7.2 %copy.34 = f32[2048,1024]{0,1:T(8,128)} copy(bf16[2048,1024]{1,0:T(8,128)(2,1)} %bitcast.280) | data formatting | bytes 12582912 | tf_op jit(solution)/shard_map/convert_element_type | solution.py:64
  124.7 4.1 multiply_convert_fusion
  128.9 2.4 fusion.26
  131.2 1.3 copy-done.8
  132.6 5.6 %convolution_bitcast_fusion = f32[2048,1024]{0,1:T(8,128)} fusion(bf16[512,2048]{1,0:T(8,128)(2,1)S(1)} %copy-done.72, f32[1024,512]{1,0:T(8,128)S(1)} %fusion.26), kind=kOutput, calls=%fused_computation.58 | convolution fusion | flops 2150105088 | bytes 12582912 | tf_op jit(solution)/shard_map/dot_general | solution.py:79
  139.0 101.9 %reduce-scatter.3.cloned.1.call-done = f32[128,1024]{0,1:T(8,128)} async-done(((f32[2048,1024]{0,1:T(8,128)}), f32[128,1024]{0,1:T(8,128)}) %reduce-scatter.3.cloned.1.call-update) | async-done | bytes 524304 | tf_op jit(solution)/shard_map/reduce_scatter | solution.py:78
  240.9 2.6 fusion.15
  243.5 91.6 %all-reduce.101.cloned.1.call-done = f32[1024,150]{0,1:T(8,128)} async-done(((f32[1024,150]{0,1:T(8,128)}), f32[1024,150]{0,1:T(8,128)}) %all-reduce.101.cloned.1.call-update) | async-done | bytes 614416 | tf_op jit(solution)/shard_map/psum | solution.py:88
  335.2 1.1 reduce_max.9
  336.3 1.2 select_reduce_fusion
  337.5 1.7 fusion.16
  339.2 1.0 copy.31
  340.2 2.5 multiply_reduce_fusion.2
  342.8 53.7 %all-gather.2.cloned.1.call-done = bf16[2048,1024]{0,1:T(8,128)(2,1)} async-done(((bf16[128,1024]{0,1:T(8,128)(2,1)}), bf16[2048,1024]{0,1:T(8,128)(2,1)}) %all-gather.2.cloned.1.call-update) | async-done | bytes 4194320 | tf_op jit(solution)/shard_map/all_gather | solution.py:103
  396.5 6.5 %fusion.8 = bf16[512,1024]{0,1:T(8,128)(2,1)S(1)} fusion(f32[1024,512]{1,0:T(8,128)} %copy-done.8, bf16[2048,1024]{0,1:T(8,128)(2,1)} %all-gather.2.cloned.1.call-done, bf16[512,2048]{1,0:T(8,128)(2,1)} %param.13), kind=kOutput, calls=%fused_computation.66 | convolution fusion | flops 2152726528 | bytes 9437184 | tf_op jit(solution)/shard_map/dot_general | solution.py:105
  403.0 6.0 %fusion.2 = (f32[1024]{0:T(1024)S(1)}, f32[1024,2048]{1,0:T(8,128)S(1)}) fusion(f32[2048,1024]{0,1:T(8,128)} %copy.34, f32[2048]{0:T(1024)S(1)} %copy-done.27, f32[1024]{0:T(1024)S(1)} %add_rsqrt_fusion, f32[1024]{0:T(1024)S(1)} %broadcast_multiply_fusion.51, bf16[512,1024]{0,1:T(8,128)(2,1)S(1)} %fusion.8, bf16[512,2048]{1,0:T(8,128)(2,1)S(1)} %copy-done), kind=kOutput, calls=%fused_computation.5 | convolution fusion | flops 2157968384 | bytes 19943424 | tf_op jit(solution)/shard_map/dot_general | solution.py:113
  409.7 5.2 fusion.1
  416.3 1.5 fusion.14
  417.8 7.0 %fusion.27 = f32[512,2048]{1,0:T(8,128)} fusion(bf16[512,1024]{0,1:T(8,128)(2,1)S(1)} %copy-done.7, bf16[2048,1024]{0,1:T(8,128)(2,1)} %copy-done.3), kind=kOutput, calls=%fused_computation.275 | convolution fusion | flops 2147483648 | bytes 9437184 | tf_op jit(solution)/shard_map/dot_general | solution.py:110
  424.9 4.5 fusion.23
  429.5 88.7 %reduce-scatter.5.cloned.1.call-done = f32[128,1024]{0,1:T(8,128)} async-done(((f32[2048,1024]{0,1:T(8,128)}), f32[128,1024]{0,1:T(8,128)}) %reduce-scatter.5.cloned.1.call-update) | async-done | bytes 524304 | tf_op jit(solution)/shard_map/reduce_scatter | solution.py:122
  518.3 2.8 broadcast_multiply_fusion.2
  521.2 1.1 broadcast_multiply_fusion.1
  522.3 2.4 broadcast_multiply_fusion
  524.7 5.8 %pad_add_fusion = f32[128,38,38]{0,2,1:T(8,128)S(1)} fusion(f32[128,32,32]{0,2,1:T(8,128)S(1)} %get-tuple-element.66, f32[128,32,32]{0,2,1:T(8,128)S(1)} %get-tuple-element.67, f32[128,32,32]{0,2,1:T(8,128)S(1)} %get-tuple-element.68, f32[128,32,32]{0,2,1:T(8,128)S(1)} %get-tuple-element.69, f32[128,32,32]{0,2,1:T(8,128)S(1)} %get-tuple-element.70, ...), kind=kLoop, calls=%fused_computation.73 | loop fusion | flops 7762944 | bytes 23283712 | tf_op jit(solution)/shard_map/transpose(jvp())/add_any | solution.py:29
  530.5 3.1 pad_add_fusion.1
  533.5 2.1 copy.32
  535.6 2.1 add.464
  538.4 1.4 multiply_reduce_fusion.50
  539.8 1.4 multiply_reduce_fusion.51
  (192 shorter events, 15.1 us)
Async XLA Ops:
  7.2 121.7 %copy-start = (bf16[512,2048]{1,0:T(8,128)(2,1)S(1)}, bf16[512,2048]{1,0:T(8,128)(2,1)}, u32[]{:S(2)}) copy-start(bf16[512,2048]{1,0:T(8,128)(2,1)} %param.12) | copy-start | bytes 6291460
  7.2 233.7 %reduce-scatter.3.cloned.1.call-start = ((), (), s32[]{:S(2)}) async-start(), calls=%async_computation.2 | async-start | bytes 8912896 | tf_op jit(solution)/shard_map/reduce_scatter | solution.py:78
  10.3 67.8 %copy-start.28 = (f32[128]{0:T(128)}, f32[128]{0:T(128)S(1)}, u32[]{:S(2)}) copy-start(f32[128]{0:T(128)S(1)} %get-tuple-element.133) | copy-start | bytes 1540
  10.3 91.3 %copy-start.30 = (f32[128]{0:T(128)}, f32[128]{0:T(128)S(1)}, u32[]{:S(2)}) copy-start(f32[128]{0:T(128)S(1)} %get-tuple-element.134) | copy-start | bytes 1540
  10.4 91.3 %copy-start.32 = (f32[128]{0:T(128)}, f32[128]{0:T(128)S(1)}, u32[]{:S(2)}) copy-start(f32[128]{0:T(128)S(1)} %get-tuple-element.135) | copy-start | bytes 1540
  10.4 91.3 %copy-start.34 = (f32[128]{0:T(128)}, f32[128]{0:T(128)S(1)}, u32[]{:S(2)}) copy-start(f32[128]{0:T(128)S(1)} %get-tuple-element.136) | copy-start | bytes 1540
  10.4 91.2 %copy-start.36 = (f32[128]{0:T(128)}, f32[128]{0:T(128)S(1)}, u32[]{:S(2)}) copy-start(f32[128]{0:T(128)S(1)} %get-tuple-element.137) | copy-start | bytes 1540
  10.4 91.2 %copy-start.38 = (f32[128]{0:T(128)}, f32[128]{0:T(128)S(1)}, u32[]{:S(2)}) copy-start(f32[128]{0:T(128)S(1)} %get-tuple-element.138) | copy-start | bytes 1540
  10.4 91.2 %copy-start.40 = (f32[128]{0:T(128)}, f32[128]{0:T(128)S(1)}, u32[]{:S(2)}) copy-start(f32[128]{0:T(128)S(1)} %get-tuple-element.139) | copy-start | bytes 1540
  16.7 9.7 %collective-permute-start = (bf16[128,1024]{1,0:T(8,128)(2,1)}, bf16[128,1024]{1,0:T(8,128)(2,1)S(1)}, u32[]{:S(2)}, u32[]{:S(2)}) collective-permute-start(bf16[128,1024]{1,0:T(8,128)(2,1)} %copy.27), channel_id=1, source_target_pairs={{0,1},{1,2},{2,3},{3,4},{4,5},{5,6},{6,7},{7,8},{8,9},{9,10},{10,1... | collective-permute-start | bytes 786440 | tf_op jit(solution)/shard_map/ppermute | solution.py:56
  26.4 51.6 %copy-start.13 = (bf16[128,1024]{1,0:T(8,128)(2,1)}, bf16[128,1024]{1,0:T(8,128)(2,1)S(1)}, u32[]{:S(2)}) copy-start(bf16[128,1024]{1,0:T(8,128)(2,1)S(1)} %collective-permute-done) | copy-start | bytes 786436
  26.4 8.5 %collective-permute-start.1 = (bf16[128,1024]{1,0:T(8,128)(2,1)S(1)}, bf16[128,1024]{1,0:T(8,128)(2,1)S(1)}, u32[]{:S(2)}, u32[]{:S(2)}) collective-permute-start(bf16[128,1024]{1,0:T(8,128)(2,1)S(1)} %collective-permute-done), channel_id=1, source_target_pairs={{0,1},{1,2},{2,3},{3,4},{4,5},{5,6},{6,7},{7,8},{8,9},{9,10},{10,1... | collective-permute-start | bytes 786440 | tf_op jit(solution)/shard_map/ppermute | solution.py:56
  26.4 8.6 %collective-permute-start.8 = (bf16[128,1024]{1,0:T(8,128)(2,1)}, bf16[128,1024]{1,0:T(8,128)(2,1)S(1)}, u32[]{:S(2)}, u32[]{:S(2)}) collective-permute-start(bf16[128,1024]{1,0:T(8,128)(2,1)} %copy.27), channel_id=1, source_target_pairs={{1,0},{2,1},{3,2},{4,3},{5,4},{6,5},{7,6},{8,7},{9,8},{10,9},{11,1... | collective-permute-start | bytes 786440 | tf_op jit(solution)/shard_map/ppermute | solution.py:58
  34.9 9.4 %copy-start.16 = (bf16[128,1024]{1,0:T(8,128)(2,1)}, bf16[128,1024]{1,0:T(8,128)(2,1)S(1)}, u32[]{:S(2)}) copy-start(bf16[128,1024]{1,0:T(8,128)(2,1)S(1)} %collective-permute-done.1) | copy-start | bytes 786436
  34.9 8.6 %collective-permute-start.2 = (bf16[128,1024]{1,0:T(8,128)(2,1)S(1)}, bf16[128,1024]{1,0:T(8,128)(2,1)S(1)}, u32[]{:S(2)}, u32[]{:S(2)}) collective-permute-start(bf16[128,1024]{1,0:T(8,128)(2,1)S(1)} %collective-permute-done.1), channel_id=1, source_target_pairs={{0,1},{1,2},{2,3},{3,4},{4,5},{5,6},{6,7},{7,8},{8,9},{9,10},{10,1... | collective-permute-start | bytes 786440 | tf_op jit(solution)/shard_map/ppermute | solution.py:56
  35.7 8.5 %collective-permute-start.9 = (bf16[128,1024]{1,0:T(8,128)(2,1)S(1)}, bf16[128,1024]{1,0:T(8,128)(2,1)S(1)}, u32[]{:S(2)}, u32[]{:S(2)}) collective-permute-start(bf16[128,1024]{1,0:T(8,128)(2,1)S(1)} %collective-permute-done.8), channel_id=1, source_target_pairs={{1,0},{2,1},{3,2},{4,3},{5,4},{6,5},{7,6},{8,7},{9,8},{10,9},{11,1... | collective-permute-start | bytes 786440 | tf_op jit(solution)/shard_map/ppermute | solution.py:58
  43.5 9.4 %copy-start.19 = (bf16[128,1024]{1,0:T(8,128)(2,1)}, bf16[128,1024]{1,0:T(8,128)(2,1)S(1)}, u32[]{:S(2)}) copy-start(bf16[128,1024]{1,0:T(8,128)(2,1)S(1)} %collective-permute-done.2) | copy-start | bytes 786436
  43.5 8.6 %collective-permute-start.3 = (bf16[128,1024]{1,0:T(8,128)(2,1)S(1)}, bf16[128,1024]{1,0:T(8,128)(2,1)S(1)}, u32[]{:S(2)}, u32[]{:S(2)}) collective-permute-start(bf16[128,1024]{1,0:T(8,128)(2,1)S(1)} %collective-permute-done.2), channel_id=1, source_target_pairs={{0,1},{1,2},{2,3},{3,4},{4,5},{5,6},{6,7},{7,8},{8,9},{9,10},{10,1... | collective-permute-start | bytes 786440 | tf_op jit(solution)/shard_map/ppermute | solution.py:56
  44.2 8.6 %collective-permute-start.10 = (bf16[128,1024]{1,0:T(8,128)(2,1)S(1)}, bf16[128,1024]{1,0:T(8,128)(2,1)S(1)}, u32[]{:S(2)}, u32[]{:S(2)}) collective-permute-start(bf16[128,1024]{1,0:T(8,128)(2,1)S(1)} %collective-permute-done.9), channel_id=1, source_target_pairs={{1,0},{2,1},{3,2},{4,3},{5,4},{6,5},{7,6},{8,7},{9,8},{10,9},{11,1... | collective-permute-start | bytes 786440 | tf_op jit(solution)/shard_map/ppermute | solution.py:58
  52.1 18.7 %copy-start.24 = (bf16[128,1024]{1,0:T(8,128)(2,1)}, bf16[128,1024]{1,0:T(8,128)(2,1)S(1)}, u32[]{:S(2)}) copy-start(bf16[128,1024]{1,0:T(8,128)(2,1)S(1)} %collective-permute-done.3) | copy-start | bytes 786436
  52.1 8.6 %collective-permute-start.4 = (bf16[128,1024]{1,0:T(8,128)(2,1)S(1)}, bf16[128,1024]{1,0:T(8,128)(2,1)S(1)}, u32[]{:S(2)}, u32[]{:S(2)}) collective-permute-start(bf16[128,1024]{1,0:T(8,128)(2,1)S(1)} %collective-permute-done.3), channel_id=1, source_target_pairs={{0,1},{1,2},{2,3},{3,4},{4,5},{5,6},{6,7},{7,8},{8,9},{9,10},{10,1... | collective-permute-start | bytes 786440 | tf_op jit(solution)/shard_map/ppermute | solution.py:56
  52.9 8.6 %collective-permute-start.11 = (bf16[128,1024]{1,0:T(8,128)(2,1)S(1)}, bf16[128,1024]{1,0:T(8,128)(2,1)S(1)}, u32[]{:S(2)}, u32[]{:S(2)}) collective-permute-start(bf16[128,1024]{1,0:T(8,128)(2,1)S(1)} %collective-permute-done.10), channel_id=1, source_target_pairs={{1,0},{2,1},{3,2},{4,3},{5,4},{6,5},{7,6},{8,7},{9,8},{10,9},{11,1... | collective-permute-start | bytes 786440 | tf_op jit(solution)/shard_map/ppermute | solution.py:58
  60.7 14.9 %copy-start.25 = (bf16[128,1024]{1,0:T(8,128)(2,1)}, bf16[128,1024]{1,0:T(8,128)(2,1)S(1)}, u32[]{:S(2)}) copy-start(bf16[128,1024]{1,0:T(8,128)(2,1)S(1)} %collective-permute-done.4) | copy-start | bytes 786436
  60.7 8.6 %collective-permute-start.5 = (bf16[128,1024]{1,0:T(8,128)(2,1)S(1)}, bf16[128,1024]{1,0:T(8,128)(2,1)S(1)}, u32[]{:S(2)}, u32[]{:S(2)}) collective-permute-start(bf16[128,1024]{1,0:T(8,128)(2,1)S(1)} %collective-permute-done.4), channel_id=1, source_target_pairs={{0,1},{1,2},{2,3},{3,4},{4,5},{5,6},{6,7},{7,8},{8,9},{9,10},{10,1... | collective-permute-start | bytes 786440 | tf_op jit(solution)/shard_map/ppermute | solution.py:56
  62.2 8.6 %collective-permute-start.12 = (bf16[128,1024]{1,0:T(8,128)(2,1)S(1)}, bf16[128,1024]{1,0:T(8,128)(2,1)}, u32[]{:S(2)}, u32[]{:S(2)}) collective-permute-start(bf16[128,1024]{1,0:T(8,128)(2,1)S(1)} %collective-permute-done.11), channel_id=1, source_target_pairs={{1,0},{2,1},{3,2},{4,3},{5,4},{6,5},{7,6},{8,7},{9,8},{10,9},{11,1... | collective-permute-start | bytes 786440 | tf_op jit(solution)/shard_map/ppermute | solution.py:58
  69.3 8.7 %copy-start.26 = (bf16[128,1024]{1,0:T(8,128)(2,1)}, bf16[128,1024]{1,0:T(8,128)(2,1)S(1)}, u32[]{:S(2)}) copy-start(bf16[128,1024]{1,0:T(8,128)(2,1)S(1)} %collective-permute-done.5) | copy-start | bytes 786436
  69.3 8.7 %collective-permute-start.6 = (bf16[128,1024]{1,0:T(8,128)(2,1)S(1)}, bf16[128,1024]{1,0:T(8,128)(2,1)}, u32[]{:S(2)}, u32[]{:S(2)}) collective-permute-start(bf16[128,1024]{1,0:T(8,128)(2,1)S(1)} %collective-permute-done.5), channel_id=1, source_target_pairs={{0,1},{1,2},{2,3},{3,4},{4,5},{5,6},{6,7},{7,8},{8,9},{9,10},{10,1... | collective-permute-start | bytes 786440 | tf_op jit(solution)/shard_map/ppermute | solution.py:56
  70.8 9.0 %collective-permute-start.13 = (bf16[128,1024]{1,0:T(8,128)(2,1)}, bf16[128,1024]{1,0:T(8,128)(2,1)}, u32[]{:S(2)}, u32[]{:S(2)}) collective-permute-start(bf16[128,1024]{1,0:T(8,128)(2,1)} %collective-permute-done.12), channel_id=1, source_target_pairs={{1,0},{2,1},{3,2},{4,3},{5,4},{6,5},{7,6},{8,7},{9,8},{10,9},{11,1... | collective-permute-start | bytes 786440 | tf_op jit(solution)/shard_map/ppermute | solution.py:58
  78.0 8.8 %collective-permute-start.7 = (bf16[128,1024]{1,0:T(8,128)(2,1)}, bf16[128,1024]{1,0:T(8,128)(2,1)}, u32[]{:S(2)}, u32[]{:S(2)}) collective-permute-start(bf16[128,1024]{1,0:T(8,128)(2,1)} %collective-permute-done.6), channel_id=1, source_target_pairs={{0,1},{1,2},{2,3},{3,4},{4,5},{5,6},{6,7},{7,8},{8,9},{9,10},{10,1... | collective-permute-start | bytes 786440 | tf_op jit(solution)/shard_map/ppermute | solution.py:56
  78.2 22.7 %copy-start.15 = (bf16[128,1024]{1,0:T(8,128)(2,1)S(1)}, bf16[128,1024]{1,0:T(8,128)(2,1)}, u32[]{:S(2)}) copy-start(bf16[128,1024]{1,0:T(8,128)(2,1)} %copy-done.14) | copy-start | bytes 786436
  78.2 23.5 %copy-start.18 = (bf16[128,1024]{1,0:T(8,128)(2,1)S(1)}, bf16[128,1024]{1,0:T(8,128)(2,1)}, u32[]{:S(2)}) copy-start(bf16[128,1024]{1,0:T(8,128)(2,1)} %copy-done.17) | copy-start | bytes 786436
  78.2 24.2 %copy-start.21 = (bf16[128,1024]{1,0:T(8,128)(2,1)S(1)}, bf16[128,1024]{1,0:T(8,128)(2,1)}, u32[]{:S(2)}) copy-start(bf16[128,1024]{1,0:T(8,128)(2,1)} %copy-done.20) | copy-start | bytes 786436
  78.2 24.9 %copy-start.23 = (bf16[128,1024]{1,0:T(8,128)(2,1)S(1)}, bf16[128,1024]{1,0:T(8,128)(2,1)}, u32[]{:S(2)}) copy-start(bf16[128,1024]{1,0:T(8,128)(2,1)} %copy-done.22) | copy-start | bytes 786436
  79.8 27.4 %collective-permute-start.14 = (bf16[128,1024]{1,0:T(8,128)(2,1)}, bf16[128,1024]{1,0:T(8,128)(2,1)S(1)}, u32[]{:S(2)}, u32[]{:S(2)}) collective-permute-start(bf16[128,1024]{1,0:T(8,128)(2,1)} %collective-permute-done.13), channel_id=1, source_target_pairs={{1,0},{2,1},{3,2},{4,3},{5,4},{6,5},{7,6},{8,7},{9,8},{10,9},{11,1... | collective-permute-start | bytes 786440 | tf_op jit(solution)/shard_map/ppermute | solution.py:58
  117.5 7.2 %copy-start.27 = (f32[2048]{0:T(1024)S(1)}, f32[2048]{0:T(1024)}, u32[]{:S(2)}) copy-start(f32[2048]{0:T(1024)} %param.10) | copy-start | bytes 24580
  138.2 198.1 %copy-start.68 = (s32[1024]{0:T(1024)S(1)}, s32[1024]{0:T(1024)}, u32[]{:S(2)}) copy-start(s32[1024]{0:T(1024)} %param.15) | copy-start | bytes 12292
  138.2 197.0 %all-reduce.101.cloned.1.call-start = ((), (), s32[]{:S(2)}) async-start(), calls=%async_computation.3 | async-start | bytes 1245184 | tf_op jit(solution)/shard_map/psum | solution.py:88
  139.0 104.5 %copy-start.70 = (f32[128]{0:T(128)}, f32[128]{0:T(128)S(1)}, u32[]{:S(2)}) copy-start(f32[128]{0:T(128)S(1)} %dynamic_slice.7) | copy-start | bytes 1540
  243.5 153.1 %all-gather.2.cloned.1.call-start = ((), (), s32[]{:S(2)}) async-start(), calls=%async_computation.4 | async-start | bytes 4456448 | tf_op jit(solution)/shard_map/all_gather | solution.py:103
  339.2 63.8 %copy-start.11 = (f32[128,1024]{1,0:T(8,128)}, f32[128,1024]{1,0:T(8,128)S(1)}, u32[]{:S(2)}) copy-start(f32[128,1024]{1,0:T(8,128)S(1)} %fusion.16) | copy-start | bytes 1572868
  342.8 175.4 %reduce-scatter.5.cloned.1.call-start = ((), (), s32[]{:S(2)}) async-start(), calls=%async_computation.5 | async-start | bytes 8912896 | tf_op jit(solution)/shard_map/reduce_scatter | solution.py:122
  396.5 13.2 %slice-start = ((s8[8388608]{0:T(1024)(128)(4,1)}), s8[4194304]{0:T(1024)(128)(4,1)S(1)}, s32[]{:S(2)}) async-start(s8[8388608]{0:T(1024)(128)(4,1)} %bitcast.278), calls=%async_computation.6 | async-start | bytes 8388608
  417.8 7.0 %copy-start.9 = (f32[1024,512]{1,0:T(8,128)S(1)}, f32[1024,512]{1,0:T(8,128)}, u32[]{:S(2)}) copy-start(f32[1024,512]{1,0:T(8,128)} %copy-done.8) | copy-start | bytes 6291460
  424.8 93.4 %copy-start.43 = (f32[128]{0:T(128)S(1)}, f32[128]{0:T(128)}, u32[]{:S(2)}) copy-start(f32[128]{0:T(128)} %copy-done.42) | copy-start | bytes 1540
  424.8 93.4 %copy-start.45 = (f32[128]{0:T(128)S(1)}, f32[128]{0:T(128)}, u32[]{:S(2)}) copy-start(f32[128]{0:T(128)} %copy-done.44) | copy-start | bytes 1540
  424.8 93.4 %copy-start.47 = (f32[128]{0:T(128)S(1)}, f32[128]{0:T(128)}, u32[]{:S(2)}) copy-start(f32[128]{0:T(128)} %copy-done.46) | copy-start | bytes 1540
  424.8 93.4 %copy-start.49 = (f32[128]{0:T(128)S(1)}, f32[128]{0:T(128)}, u32[]{:S(2)}) copy-start(f32[128]{0:T(128)} %copy-done.48) | copy-start | bytes 1540
  424.8 93.4 %copy-start.51 = (f32[128]{0:T(128)S(1)}, f32[128]{0:T(128)}, u32[]{:S(2)}) copy-start(f32[128]{0:T(128)} %copy-done.50) | copy-start | bytes 1540
  424.8 93.4 %copy-start.53 = (f32[128]{0:T(128)S(1)}, f32[128]{0:T(128)}, u32[]{:S(2)}) copy-start(f32[128]{0:T(128)} %copy-done.52) | copy-start | bytes 1540
  424.8 93.4 %copy-start.55 = (f32[128]{0:T(128)S(1)}, f32[128]{0:T(128)}, u32[]{:S(2)}) copy-start(f32[128]{0:T(128)} %copy-done.54) | copy-start | bytes 1540
  424.8 93.4 %copy-start.57 = (f32[128]{0:T(128)S(1)}, f32[128]{0:T(128)}, u32[]{:S(2)}) copy-start(f32[128]{0:T(128)} %copy-done.56) | copy-start | bytes 1540
  424.9 93.4 %copy-start.59 = (f32[128]{0:T(128)S(1)}, f32[128]{0:T(128)}, u32[]{:S(2)}) copy-start(f32[128]{0:T(128)} %copy-done.58) | copy-start | bytes 1540
  424.9 93.4 %copy-start.61 = (f32[128]{0:T(128)S(1)}, f32[128]{0:T(128)}, u32[]{:S(2)}) copy-start(f32[128]{0:T(128)} %copy-done.60) | copy-start | bytes 1540
  424.9 93.4 %copy-start.63 = (f32[128]{0:T(128)S(1)}, f32[128]{0:T(128)}, u32[]{:S(2)}) copy-start(f32[128]{0:T(128)} %copy-done.62) | copy-start | bytes 1540
  424.9 93.4 %copy-start.65 = (f32[128]{0:T(128)S(1)}, f32[128]{0:T(128)}, u32[]{:S(2)}) copy-start(f32[128]{0:T(128)} %copy-done.64) | copy-start | bytes 1540
  424.9 93.4 %copy-start.67 = (f32[128]{0:T(128)S(1)}, f32[128]{0:T(128)}, u32[]{:S(2)}) copy-start(f32[128]{0:T(128)} %copy-done.66) | copy-start | bytes 1540
  429.4 91.7 %copy-start.29 = (f32[128]{0:T(128)S(1)}, f32[128]{0:T(128)}, u32[]{:S(2)}) copy-start(f32[128]{0:T(128)} %copy-done.28) | copy-start | bytes 1540
  429.4 91.7 %copy-start.31 = (f32[128]{0:T(128)S(1)}, f32[128]{0:T(128)}, u32[]{:S(2)}) copy-start(f32[128]{0:T(128)} %copy-done.30) | copy-start | bytes 1540
  429.4 91.7 %copy-start.33 = (f32[128]{0:T(128)S(1)}, f32[128]{0:T(128)}, u32[]{:S(2)}) copy-start(f32[128]{0:T(128)} %copy-done.32) | copy-start | bytes 1540
  429.4 91.7 %copy-start.35 = (f32[128]{0:T(128)S(1)}, f32[128]{0:T(128)}, u32[]{:S(2)}) copy-start(f32[128]{0:T(128)} %copy-done.34) | copy-start | bytes 1540
  429.4 91.7 %copy-start.37 = (f32[128]{0:T(128)S(1)}, f32[128]{0:T(128)}, u32[]{:S(2)}) copy-start(f32[128]{0:T(128)} %copy-done.36) | copy-start | bytes 1540
  429.5 91.7 %copy-start.39 = (f32[128]{0:T(128)S(1)}, f32[128]{0:T(128)}, u32[]{:S(2)}) copy-start(f32[128]{0:T(128)} %copy-done.38) | copy-start | bytes 1540
  429.5 91.7 %copy-start.41 = (f32[128]{0:T(128)S(1)}, f32[128]{0:T(128)}, u32[]{:S(2)}) copy-start(f32[128]{0:T(128)} %copy-done.40) | copy-start | bytes 1540
  530.5 11.6 %copy-start.1 = (bf16[512,2048]{1,0:T(8,128)(2,1)S(1)}, bf16[512,2048]{1,0:T(8,128)(2,1)}, u32[]{:S(2)}) copy-start(bf16[512,2048]{1,0:T(8,128)(2,1)} %param.12) | copy-start | bytes 6291460
  (30 other events, 137.4 us)
Sparse Core Ops, SparseCore 0:
  138.3 102.5 reduce-scatter.2
  244.9 90.2 all-reduce.100
  342.9 53.5 all-gather.1
  415.1 103.0 reduce-scatter.4
